TPU v7x, 32 devices: a whole 2x2x4 slice. The times are simulated.
32 devices in a mesh: tx: 8 (over y, x, core), ty: 4 (over z).
Axes of the slice: x: 2, y: 2, z: 4, core: 2. Of those that a mesh axis runs over, the one named last changes fastest.
Arguments:
- volume: bfloat16 [256, 128, 16, 64], P('tx', 'ty'), may hold values from -6 to 6
- first_weight: bfloat16 [2, 2, 2, 64, 128], replicated, may hold values from -0.375 to 0.375
- first_bias: float32 [128], replicated, may hold values from -1.5 to 1.5
- second_weight: bfloat16 [2, 2, 2, 128, 256], replicated, may hold values from -0.25 to 0.25
- second_bias: float32 [256], replicated, may hold values from -1.5 to 1.5
- inner_weight: bfloat16 [3, 3, 3, 256, 256], replicated, may hold values from -0.109375 to 0.109375
- inner_bias: float32 [256], replicated, may hold values from -1.5 to 1.5
- outer_weight: bfloat16 [3, 3, 3, 256, 256], replicated, may hold values from -0.109375 to 0.109375
- outer_bias: float32 [256], replicated, may hold values from -1.5 to 1.5
Outputs:
- encoded: bfloat16 [64, 32, 4, 256], P('tx', 'ty')
All inputs are finite; a program needn't handle non-finite values.
Results may differ from a plain program's by a relative error of at most 0.0058.
Values may be sent and summed in bfloat16 or wider, within the bound.
A program may use at most 64 MiB of HBM per device.

v0:
```python
import jax
import jax.numpy as jnp
from jax import lax
from jax.experimental import pallas as pl
from jax.experimental.pallas import tpu as pltpu
from jax.sharding import PartitionSpec as P

MESSAGES = (
    (-1, 0, 0), (1, 0, 1),
    (-1, -1, 0), (-1, 1, 0), (0, -1, 0), (0, 1, 0),
    (1, -1, 1), (1, 1, 1), (0, -1, 1), (0, 1, 1),
)
PARTNER = (1, 0, 7, 6, 5, 4, 3, 2, 9, 8)
FIRST = (2, 3, 4, 5, 0)
SECOND = (6, 7, 8, 9, 1)
NEIGHBOURS = (0, 1, 2, 3, 4, 5, 6, 7)
BF = jnp.bfloat16
F32 = jnp.float32


def leaky(values):
    return jnp.where(values > 0, values, 0.01 * values)


def kernel(
    volume, w1, b1, w2, b2, wi, bi, wo, bo,
    out,
    vbuf, w1b, w2b, wib, wob, b1b, b2b, bib, bob,
    sums, blocks, halo, inner, edge_out, edge_in, corner_out, corner_in,
    load_sem, send_sem, recv_sem,
):
    ix, iy = lax.axis_index("tx"), lax.axis_index("ty")
    nx, ny = lax.axis_size("tx"), lax.axis_size("ty")
    groups_x, groups_y = halo.shape[1] - 4, halo.shape[2] - 4
    half = groups_x * groups_y * 8

    def exists(d):
        dx, dy, _ = MESSAGES[d]
        test = None
        for delta, i, n in ((dx, ix, nx), (dy, iy, ny)):
            if delta:
                one = i >= 1 if delta < 0 else i <= n - 2
                test = one if test is None else jnp.logical_and(test, one)
        return test

    def device(d):
        return {"tx": ix + MESSAGES[d][0], "ty": iy + MESSAGES[d][1]}

    loads = []

    def load(src, dst):
        copy = pltpu.make_async_copy(src, dst, load_sem.at[len(loads)])
        copy.start()
        loads.append(copy)
        return copy

    load_w1, load_b1 = load(w1, w1b), load(b1, b1b)
    load_v = [load(volume.at[pl.ds(8 * i, 8)], vbuf.at[i]) for i in range(groups_x)]
    load_w2, load_b2 = load(w2, w2b), load(b2, b2b)
    load_bi, load_bo = load(bi, bib), load(bo, bob)
    load_wi = {a: load(wi.at[a], wib.at[a]) for a in (1, 0, 2)}
    load_wo = {a: load(wo.at[a], wob.at[a]) for a in (1, 0, 2)}

    barrier = pltpu.get_barrier_semaphore()
    count = 0
    for d in NEIGHBOURS:
        count = count + exists(d).astype(jnp.int32)

        @pl.when(exists(d))
        def _():
            pl.semaphore_signal(
                barrier, inc=1, device_id=device(d), device_id_type=pl.DeviceIdType.MESH
            )

    halo[...] = jnp.zeros_like(halo)

    load_w1.wait()
    load_b1.wait()
    w1cat = jnp.concatenate(
        [
            jnp.concatenate([w1b[p, q, 0], w1b[p, q, 1]], axis=1)
            for p in range(2)
            for q in range(2)
        ],
        axis=0,
    )
    rows_y = 2 * groups_y
    bias1 = b1b[...]
    def first(i):
        load_v[i].wait()
        for xp in range(2):
            slabs = [
                vbuf[i, 4 * xp + j].reshape(rows_y, 4, 16, 64) for j in range(4)
            ]
            for pc in range(2):
                for qc in range(2):
                    lhs = jnp.concatenate(
                        [
                            slabs[2 * pc + p][:, 2 * qc + q].reshape(rows_y * 16, 64)
                            for p in range(2)
                            for q in range(2)
                        ],
                        axis=1,
                    )
                    slot = (i * 2 + xp) * 4 + pc * 2 + qc
                    both = jnp.dot(lhs, w1cat, preferred_element_type=F32)
                    sums[slot, 0] = both[:, 0:128]
                    sums[slot, 1] = both[:, 128:256]
            for pc in range(2):
                for qc in range(2):
                    slot = (i * 2 + xp) * 4 + pc * 2 + qc
                    for rc in range(2):
                        even = sums[slot, 0, pl.ds(2 * rc, 4 * rows_y, stride=4)]
                        odd = sums[slot, 1, pl.ds(2 * rc + 1, 4 * rows_y, stride=4)]
                        finer = leaky(even + odd + bias1).astype(BF)
                        k = (pc * 2 + qc) * 2 + rc
                        row = (i * 2 + xp) * 4 * rows_y
                        blocks[row : row + 4 * rows_y, k * 128 : k * 128 + 128] = finer

    def copy_of(d, incoming):
        slot = d if incoming else PARTNER[d]
        if d < 2:
            src, dst = edge_out.at[d], edge_in.at[slot]
        else:
            src, dst = corner_out.at[d - 2], corner_in.at[slot - 2]
        return pltpu.make_async_remote_copy(
            src_ref=src,
            dst_ref=dst,
            send_sem=send_sem.at[d],
            recv_sem=recv_sem.at[slot],
            device_id=device(d),
            device_id_type=pl.DeviceIdType.MESH,
        )

    def landed(d):
        dx, dy, h = MESSAGES[d]
        if dx:
            px = slice(0, 2) if dx < 0 else slice(groups_x + 2, groups_x + 4)
        else:
            px = slice(2 + 2 * h, 4 + 2 * h)
        if dy:
            return px, slice(0, 2) if dy < 0 else slice(groups_y + 2, groups_y + 4)
        return px, slice(2, 2 + groups_y)

    def second(h):
        rows = half
        total = jnp.dot(
            blocks[h * rows : h * rows + rows],
            w2b[...].reshape(8 * 128, 256),
            preferred_element_type=F32,
        )
        coarse = leaky(total + b2b[...]).astype(BF).astype(F32)
        coarse = coarse.reshape(groups_x // 2, 2, groups_y * 8, 256)
        rows = half // 2
        even_x = coarse[:, 0].reshape(rows, 256)
        odd_x = coarse[:, 1].reshape(rows, 256)
        keep = (lax.broadcasted_iota(jnp.int32, (rows, 256), 0) // 2) % 2 == 0
        parts = [
            part.reshape(groups_x // 2, groups_y, 8, 256)
            for part in (
                jnp.where(keep, even_x, pltpu.roll(odd_x, 2, 0)),
                jnp.where(keep, pltpu.roll(even_x, rows - 2, 0), odd_x),
            )
        ]
        for d in SECOND if h else FIRST:
            dy = MESSAGES[d][1]
            sy = slice(0, 2) if dy < 0 else slice(groups_y - 2, groups_y) if dy else slice(0, groups_y)
            block = jnp.concatenate([p[:, sy].reshape(-1, 256) for p in parts], axis=0).astype(BF)
            if d < 2:
                edge_out[d] = block
            else:
                corner_out[d - 2] = block

            @pl.when(exists(d))
            def _():
                copy_of(d, False).start()

        for z in range(2):
            halo[z, 2 + 2 * h : 4 + 2 * h, 2 : 2 + groups_y] = parts[z]

    per_half = groups_x // 2
    for i in range(per_half):
        first(i)
    load_w2.wait()
    load_b2.wait()
    pl.semaphore_wait(barrier, count)
    second(0)
    for i in range(per_half, groups_x):
        first(i)
    second(1)

    own = jnp.concatenate(
        [
            halo[z, 2 : 2 + groups_x, 2 : 2 + groups_y].reshape(half, 256).astype(BF)
            for z in range(2)
        ],
        axis=1,
    )
    keep = (lax.broadcasted_iota(jnp.int32, (half, 256), 0) // 2) % 2 == 0
    load_bi.wait()
    load_bo.wait()
    inner[...] = jnp.broadcast_to(bib[...].reshape(1, 1, 1, 1, 256), inner.shape)

    def both(lhs, weight, a, b):
        lower = weight[a, b, 1:3].reshape(512, 256)
        upper = weight[a, b, 0:2].reshape(512, 256)
        return (
            jnp.dot(lhs, lower, preferred_element_type=F32),
            jnp.dot(lhs, upper, preferred_element_type=F32),
        )

    for a in (1, 0, 2):
        load_wi[a].wait()
        for b in (1, 0, 2):
            for z, term in enumerate(both(own, wib, a, b)):
                inner[z, 2 - a : 2 - a + groups_x, 2 - b : 2 - b + groups_y] += term.reshape(
                    groups_x, groups_y, 8, 256
                )

    for d in FIRST + SECOND:
        px, py = landed(d)

        @pl.when(exists(d))
        def _():
            copy_of(d, True).wait_recv()
            block = (edge_in[d] if d < 2 else corner_in[d - 2]).astype(F32)
            rows = block.shape[0] // 2
            for z in range(2):
                shape = (px.stop - px.start, py.stop - py.start, 8, 256)
                halo[z, px, py] = block[z * rows : z * rows + rows].reshape(shape)

    def outside(shift, groups):
        return [i for i in range(shift, shift + groups + 2) if not 2 <= i < 2 + groups]

    for a in (1, 0, 2):
        for b in (1, 0, 2):
            pieces = [
                (slice(i, i + 1), slice(b, b + groups_y + 2)) for i in outside(a, groups_x)
            ] + [
                (slice(2, 2 + groups_x), slice(i, i + 1)) for i in outside(b, groups_y)
            ]
            lhs = jnp.concatenate(
                [
                    jnp.concatenate(
                        [halo[z, sx, sy].reshape(-1, 256) for sx, sy in pieces], axis=0
                    ).astype(BF)
                    for z in range(2)
                ],
                axis=1,
            )
            for z, term in enumerate(both(lhs, wib, a, b)):
                row = 0
                for sx, sy in pieces:
                    shape = (sx.stop - sx.start, sy.stop - sy.start, 8, 256)
                    rows = shape[0] * shape[1] * 8
                    inner[
                        z, sx.start - a : sx.stop - a, sy.start - b : sy.stop - b
                    ] += term[row : row + rows].reshape(shape)
                    row += rows

    inner[...] = leaky(inner[...]).astype(BF).astype(F32)

    @pl.when(ix == 0)
    def _():
        inner[:, 0] = jnp.zeros_like(inner[:, 0])

    @pl.when(ix == nx - 1)
    def _():
        inner[:, groups_x + 1] = jnp.zeros_like(inner[:, 0])

    @pl.when(iy == 0)
    def _():
        inner[:, :, 0] = jnp.zeros_like(inner[:, :, 0])

    @pl.when(iy == ny - 1)
    def _():
        inner[:, :, groups_y + 1] = jnp.zeros_like(inner[:, :, 0])

    totals = [
        halo[z, 2 : 2 + groups_x, 2 : 2 + groups_y].reshape(half, 256) + bob[...]
        for z in range(2)
    ]
    for a in (1, 0, 2):
        load_wo[a].wait()
        for b in (1, 0, 2):
            lhs = jnp.concatenate(
                [
                    inner[z, a : a + groups_x, b : b + groups_y].reshape(half, 256).astype(BF)
                    for z in range(2)
                ],
                axis=1,
            )
            totals = [t + term for t, term in zip(totals, both(lhs, wob, a, b))]
    lower, upper = leaky(totals[0]), leaky(totals[1])
    even_x = jnp.where(keep, lower, pltpu.roll(upper, 2, 0)).astype(BF)
    odd_x = jnp.where(keep, pltpu.roll(lower, half - 2, 0), upper).astype(BF)
    rows = groups_y * 8
    for i in range(groups_x):
        out[(2 * i) * rows : (2 * i + 1) * rows] = even_x[i * rows : (i + 1) * rows]
        out[(2 * i + 1) * rows : (2 * i + 2) * rows] = odd_x[i * rows : (i + 1) * rows]

    for d in range(10):

        @pl.when(exists(d))
        def _():
            copy_of(d, False).wait_send()


def local(
    volume,
    first_weight,
    first_bias,
    second_weight,
    second_bias,
    inner_weight,
    inner_bias,
    outer_weight,
    outer_bias,
):
    size_x, size_y, size_z, chans = volume.shape
    gx, gy = size_x // 8, size_y // 8
    cells = gx * gy * 16
    any_spec = pl.BlockSpec(memory_space=pl.ANY)
    vmem = pltpu.VMEM
    result = pl.pallas_call(
        kernel,
        out_shape=jax.ShapeDtypeStruct((cells, 256), BF),
        in_specs=[any_spec] * 9,
        out_specs=pl.BlockSpec(memory_space=pltpu.VMEM),
        scratch_shapes=[
            vmem((gx, 8, size_y, size_z, chans), BF),
            vmem(first_weight.shape, BF),
            vmem(second_weight.shape, BF),
            vmem(inner_weight.shape, BF),
            vmem(outer_weight.shape, BF),
            vmem((1, 128), F32),
            vmem((1, 256), F32),
            vmem((1, 256), F32),
            vmem((1, 256), F32),
            vmem((gx * 8, 2, gy * 32, 128), F32),
            vmem((cells, 1024), BF),
            vmem((2, gx + 4, gy + 4, 8, 256), F32),
            vmem((2, gx + 2, gy + 2, 8, 256), F32),
            vmem((2, gy * 32, 256), BF),
            vmem((2, gy * 32, 256), BF),
            vmem((8, 64, 256), BF),
            vmem((8, 64, 256), BF),
            pltpu.SemaphoreType.DMA((gx + 12,)),
            pltpu.SemaphoreType.DMA((10,)),
            pltpu.SemaphoreType.DMA((10,)),
        ],
        compiler_params=pltpu.CompilerParams(
            collective_id=0, has_side_effects=True, vmem_limit_bytes=56 * 2**20
        ),
        cost_estimate=pl.CostEstimate(
            flops=2_000_000_000, bytes_accessed=12_000_000, transcendentals=0
        ),
    )(
        volume,
        first_weight,
        first_bias.reshape(1, -1),
        second_weight,
        second_bias.reshape(1, -1),
        inner_weight,
        inner_bias.reshape(1, -1),
        outer_weight,
        outer_bias.reshape(1, -1),
    )
    return result.reshape(size_x // 4, size_y // 4, size_z // 4, 256)


def solution(mesh):
    in_specs = (P("tx", "ty", None, None), P(), P(), P(), P(), P(), P(), P(), P())
    out_specs = P("tx", "ty", None, None)
    return jax.shard_map(local, mesh=mesh, in_specs=in_specs, out_specs=out_specs, check_vma=False)
```

profile of v0, /device:TPU:0, one launch (start us, length us, event | category | flops | bytes accessed | tf_op | source)
XLA Modules:
  0.0 13.8 jit_solution(14368345707265320709)
XLA Ops:
  0.0 12.2 %shard_map.91 = bf16[256,256]{1,0:T(8,128)(2,1)} custom-call(bf16[32,32,16,64]{3,2,1,0:T(8,128)(2,1)} %volume.1, bf16[2,2,2,64,128]{4,3,2,1,0:T(8,128)(2,1)} %w1.1, f32[1,128]{1,0:T(1,128)} %bitcast.7, bf16[2,2,2,128,256]{4,3,2,1,0:T(8,128)(2,1)} %w2.1, f32[1,256]{1,0:T(1,128)} %bitcast.4, bf16[3,3,3,256,256]{4,3,2,1,0:T(8,128)(2,1)} %wi.1, ...), custom_call_target="tpu_custom_call" | custom-call | flops 2000000000 | bytes 12000000 | tf_op jit(solution)/shard_map/pallas_call | solution.py:325
  12.2 1.6 %reshape.19 = bf16[8,8,4,256]{3,2,1,0:T(4,128)(2,1)} reshape(bf16[256,256]{1,0:T(8,128)(2,1)} %shard_map.91) | data formatting | bytes 262144 | tf_op jit(solution)/shard_map/reshape | solution.py:369
where the time goes:
time: 14 us; the launch traced here: 13.8 us
  Pallas kernels  12.2 us (87%)
  local copies, waits for them, and re-layouts  1.6 us (11%)
    pallas_call x1, Pallas kernels, local(): pl.pallas_call(kernel, out_shape=jax.ShapeDtypeStruct((cells, 256), BF),...  12.2 us
    reshape x1, local copies, waits for them, and re-layouts, local(): return result.reshape(size_x // 4, size_y // 4, size_z // 4, 256)  1.6 us

commit v1 on v0

--- a/solution.py
+++ b/solution.py
@@ -296,8 +296,8 @@
     odd_x = jnp.where(keep, pltpu.roll(lower, half - 2, 0), upper).astype(BF)
     rows = groups_y * 8
     for i in range(groups_x):
-        out[(2 * i) * rows : (2 * i + 1) * rows] = even_x[i * rows : (i + 1) * rows]
-        out[(2 * i + 1) * rows : (2 * i + 2) * rows] = odd_x[i * rows : (i + 1) * rows]
+        for p, part in enumerate((even_x, odd_x)):
+            out[2 * i + p] = part[i * rows : (i + 1) * rows].reshape(2 * groups_y, 4, 256)
 
     for d in range(10):
 
@@ -324,7 +324,7 @@
     vmem = pltpu.VMEM
     result = pl.pallas_call(
         kernel,
-        out_shape=jax.ShapeDtypeStruct((cells, 256), BF),
+        out_shape=pltpu.VMEM((size_x // 4, size_y // 4, size_z // 4, 256), BF),
         in_specs=[any_spec] * 9,
         out_specs=pl.BlockSpec(memory_space=pltpu.VMEM),
         scratch_shapes=[
@@ -366,7 +366,7 @@
         outer_weight,
         outer_bias.reshape(1, -1),
     )
-    return result.reshape(size_x // 4, size_y // 4, size_z // 4, 256)
+    return result
 
 
 def solution(mesh):

time: 14 us -> 12.4 us (0.89)
  local copies, waits for them, and re-layouts: 1.6 us -> 0.66 us
  Pallas kernels: 12.2 us -> 11.6 us
    reshape x1 -> x0, local copies, waits for them, and re-layouts: 1.6 us -> none  [local(): return result.reshape(size_x // 4, size_y // 4, size_z // 4, 256)]
    unnamed x0 -> x1, local copies, waits for them, and re-layouts: none -> 0.66 us
    pallas_call x1, Pallas kernels: 12.2 us -> 11.6 us  [local(): pl.pallas_call(kernel, out_shape=pltpu.VMEM((size_x // 4, size_y // 4, si...]
where the time goes in v1:
time: 12.4 us; the launch traced here: 12.3 us
  Pallas kernels  11.6 us (94%)
  local copies, waits for them, and re-layouts  0.66 us (5%)
    pallas_call x1, Pallas kernels, local(): pl.pallas_call(kernel, out_shape=pltpu.VMEM((size_x // 4, size_y // 4, si...  11.6 us
    unnamed x1, local copies, waits for them, and re-layouts  0.66 us

profile of v1, /device:TPU:0, one launch (start us, length us, event | category | flops | bytes accessed | tf_op | source)
XLA Modules:
  0.0 12.3 jit_solution(3159191561080507234)
XLA Ops:
  0.0 11.6 %shard_map.91 = bf16[8,8,4,256]{3,2,1,0:T(4,128)(2,1)S(1)} custom-call(bf16[32,32,16,64]{3,2,1,0:T(8,128)(2,1)} %volume.1, bf16[2,2,2,64,128]{4,3,2,1,0:T(8,128)(2,1)} %w1.1, f32[1,128]{1,0:T(1,128)} %bitcast.7, bf16[2,2,2,128,256]{4,3,2,1,0:T(8,128)(2,1)} %w2.1, f32[1,256]{1,0:T(1,128)} %bitcast.4, bf16[3,3,3,256,256]{4,3,2,1,0:T(8,128)(2,1)} %wi.1, ...), custom_call_target="tpu_custom_call" | custom-call | flops 2000000000 | bytes 12000000 | tf_op jit(solution)/shard_map/pallas_call | solution.py:325
  11.6 0.7 %copy.11 = bf16[8,8,4,256]{3,2,1,0:T(4,128)(2,1)} copy(bf16[8,8,4,256]{3,2,1,0:T(4,128)(2,1)S(1)} %shard_map.91) | data formatting | bytes 262144

commit v2 on v1

--- a/solution.py
+++ b/solution.py
@@ -12,7 +12,7 @@
 )
 PARTNER = (1, 0, 7, 6, 5, 4, 3, 2, 9, 8)
 FIRST = (2, 3, 4, 5, 0)
-SECOND = (6, 7, 8, 9, 1)
+SECOND = (8, 9, 6, 7, 1)
 NEIGHBOURS = (0, 1, 2, 3, 4, 5, 6, 7)
 BF = jnp.bfloat16
 F32 = jnp.float32
@@ -26,7 +26,7 @@
     volume, w1, b1, w2, b2, wi, bi, wo, bo,
     out,
     vbuf, w1b, w2b, wib, wob, b1b, b2b, bib, bob,
-    sums, blocks, halo, inner, edge_out, edge_in, corner_out, corner_in,
+    lhs, sums, blocks, halo, inner, edge_out, edge_in, corner_out, corner_in,
     load_sem, send_sem, recv_sem,
 ):
     ix, iy = lax.axis_index("tx"), lax.axis_index("ty")
@@ -46,6 +46,17 @@
     def device(d):
         return {"tx": ix + MESSAGES[d][0], "ty": iy + MESSAGES[d][1]}
 
+    barrier = pltpu.get_barrier_semaphore()
+    count = 0
+    for d in NEIGHBOURS:
+        count = count + exists(d).astype(jnp.int32)
+
+        @pl.when(exists(d))
+        def _():
+            pl.semaphore_signal(
+                barrier, inc=1, device_id=device(d), device_id_type=pl.DeviceIdType.MESH
+            )
+
     loads = []
 
     def load(src, dst):
@@ -55,22 +66,13 @@
         return copy
 
     load_w1, load_b1 = load(w1, w1b), load(b1, b1b)
-    load_v = [load(volume.at[pl.ds(8 * i, 8)], vbuf.at[i]) for i in range(groups_x)]
+    units = vbuf.shape[0]
+    load_v = [load(volume.at[pl.ds(4 * u, 4)], vbuf.at[u]) for u in range(units // 2)]
     load_w2, load_b2 = load(w2, w2b), load(b2, b2b)
+    load_v += [load(volume.at[pl.ds(4 * u, 4)], vbuf.at[u]) for u in range(units // 2, units)]
     load_bi, load_bo = load(bi, bib), load(bo, bob)
     load_wi = {a: load(wi.at[a], wib.at[a]) for a in (1, 0, 2)}
     load_wo = {a: load(wo.at[a], wob.at[a]) for a in (1, 0, 2)}
-
-    barrier = pltpu.get_barrier_semaphore()
-    count = 0
-    for d in NEIGHBOURS:
-        count = count + exists(d).astype(jnp.int32)
-
-        @pl.when(exists(d))
-        def _():
-            pl.semaphore_signal(
-                barrier, inc=1, device_id=device(d), device_id_type=pl.DeviceIdType.MESH
-            )
 
     halo[...] = jnp.zeros_like(halo)
 
@@ -86,36 +88,34 @@
     )
     rows_y = 2 * groups_y
     bias1 = b1b[...]
-    def first(i):
-        load_v[i].wait()
-        for xp in range(2):
-            slabs = [
-                vbuf[i, 4 * xp + j].reshape(rows_y, 4, 16, 64) for j in range(4)
-            ]
-            for pc in range(2):
-                for qc in range(2):
-                    lhs = jnp.concatenate(
-                        [
-                            slabs[2 * pc + p][:, 2 * qc + q].reshape(rows_y * 16, 64)
-                            for p in range(2)
-                            for q in range(2)
-                        ],
-                        axis=1,
-                    )
-                    slot = (i * 2 + xp) * 4 + pc * 2 + qc
-                    both = jnp.dot(lhs, w1cat, preferred_element_type=F32)
-                    sums[slot, 0] = both[:, 0:128]
-                    sums[slot, 1] = both[:, 128:256]
-            for pc in range(2):
-                for qc in range(2):
-                    slot = (i * 2 + xp) * 4 + pc * 2 + qc
-                    for rc in range(2):
-                        even = sums[slot, 0, pl.ds(2 * rc, 4 * rows_y, stride=4)]
-                        odd = sums[slot, 1, pl.ds(2 * rc + 1, 4 * rows_y, stride=4)]
-                        finer = leaky(even + odd + bias1).astype(BF)
-                        k = (pc * 2 + qc) * 2 + rc
-                        row = (i * 2 + xp) * 4 * rows_y
-                        blocks[row : row + 4 * rows_y, k * 128 : k * 128 + 128] = finer
+
+    def gather(u):
+        slabs = [vbuf[u, j].reshape(rows_y, 4, 16, 64) for j in range(4)]
+        for pc in range(2):
+            for qc in range(2):
+                lhs[u % 2, pc * 2 + qc] = jnp.concatenate(
+                    [
+                        slabs[2 * pc + p][:, 2 * qc + q].reshape(rows_y * 16, 64)
+                        for p in range(2)
+                        for q in range(2)
+                    ],
+                    axis=1,
+                )
+
+    def multiply(u):
+        for k in range(4):
+            both = jnp.dot(lhs[u % 2, k], w1cat, preferred_element_type=F32)
+            sums[u * 4 + k, 0] = both[:, 0:128]
+            sums[u * 4 + k, 1] = both[:, 128:256]
+
+    def fold(u):
+        row = u * 4 * rows_y
+        for k in range(8):
+            slot, rc = u * 4 + k // 2, k % 2
+            even = sums[slot, 0, pl.ds(2 * rc, 4 * rows_y, stride=4)]
+            odd = sums[slot, 1, pl.ds(2 * rc + 1, 4 * rows_y, stride=4)]
+            finer = leaky(even + odd + bias1).astype(BF)
+            blocks[row : row + 4 * rows_y, k * 128 : k * 128 + 128] = finer
 
     def copy_of(d, incoming):
         slot = d if incoming else PARTNER[d]
@@ -178,16 +178,21 @@
         for z in range(2):
             halo[z, 2 + 2 * h : 4 + 2 * h, 2 : 2 + groups_y] = parts[z]
 
-    per_half = groups_x // 2
-    for i in range(per_half):
-        first(i)
-    load_w2.wait()
-    load_b2.wait()
-    pl.semaphore_wait(barrier, count)
-    second(0)
-    for i in range(per_half, groups_x):
-        first(i)
-    second(1)
+    for t in range(units + 2):
+        if t < units:
+            load_v[t].wait()
+            gather(t)
+        if 1 <= t <= units:
+            multiply(t - 1)
+        if 2 <= t:
+            fold(t - 2)
+        if t == units // 2 + 1:
+            load_w2.wait()
+            load_b2.wait()
+            pl.semaphore_wait(barrier, count)
+            second(0)
+        if t == units + 1:
+            second(1)
 
     own = jnp.concatenate(
         [
@@ -217,10 +222,13 @@
                     groups_x, groups_y, 8, 256
                 )
 
-    for d in FIRST + SECOND:
+    def receive(d, test=None):
         px, py = landed(d)
-
-        @pl.when(exists(d))
+        there = exists(d)
+        if test is not None:
+            there = jnp.logical_and(there, test)
+
+        @pl.when(there)
         def _():
             copy_of(d, True).wait_recv()
             block = (edge_in[d] if d < 2 else corner_in[d - 2]).astype(F32)
@@ -229,68 +237,111 @@
                 shape = (px.stop - px.start, py.stop - py.start, 8, 256)
                 halo[z, px, py] = block[z * rows : z * rows + rows].reshape(shape)
 
-    def outside(shift, groups):
-        return [i for i in range(shift, shift + groups + 2) if not 2 <= i < 2 + groups]
-
-    for a in (1, 0, 2):
-        for b in (1, 0, 2):
-            pieces = [
-                (slice(i, i + 1), slice(b, b + groups_y + 2)) for i in outside(a, groups_x)
-            ] + [
-                (slice(2, 2 + groups_x), slice(i, i + 1)) for i in outside(b, groups_y)
-            ]
-            lhs = jnp.concatenate(
-                [
-                    jnp.concatenate(
-                        [halo[z, sx, sy].reshape(-1, 256) for sx, sy in pieces], axis=0
-                    ).astype(BF)
-                    for z in range(2)
-                ],
-                axis=1,
-            )
-            for z, term in enumerate(both(lhs, wib, a, b)):
-                row = 0
-                for sx, sy in pieces:
-                    shape = (sx.stop - sx.start, sy.stop - sy.start, 8, 256)
-                    rows = shape[0] * shape[1] * 8
-                    inner[
-                        z, sx.start - a : sx.stop - a, sy.start - b : sy.stop - b
-                    ] += term[row : row + rows].reshape(shape)
-                    row += rows
-
-    inner[...] = leaky(inner[...]).astype(BF).astype(F32)
-
-    @pl.when(ix == 0)
-    def _():
-        inner[:, 0] = jnp.zeros_like(inner[:, 0])
-
-    @pl.when(ix == nx - 1)
-    def _():
-        inner[:, groups_x + 1] = jnp.zeros_like(inner[:, 0])
-
-    @pl.when(iy == 0)
-    def _():
-        inner[:, :, 0] = jnp.zeros_like(inner[:, :, 0])
-
-    @pl.when(iy == ny - 1)
-    def _():
-        inner[:, :, groups_y + 1] = jnp.zeros_like(inner[:, :, 0])
-
-    totals = [
-        halo[z, 2 : 2 + groups_x, 2 : 2 + groups_y].reshape(half, 256) + bob[...]
-        for z in range(2)
-    ]
+    core = lax.rem(ix, 2)
+
+    def side(flip):
+        def pick(even, odd):
+            return even + flip * (odd - even)
+
+        return (
+            pick(groups_x + 2, 1),
+            pick(groups_x + 3, 0),
+            pick(groups_x + 1, 0),
+            pick(groups_x, 1),
+            pick(2, 0),
+        )
+
+    near_in, far_in, ring_in, edge_in_x, tap_in = side(core)
+    near_out, far_out, ring_out, edge_out_x, tap_out = side(1 - core)
+
+    def add(a, b, pieces):
+        lhs_halo = jnp.concatenate(
+            [
+                jnp.concatenate(
+                    [halo[z, pl.ds(g, n), sy].reshape(-1, 256) for g, n, sy, _ in pieces],
+                    axis=0,
+                ).astype(BF)
+                for z in range(2)
+            ],
+            axis=1,
+        )
+        for z, term in enumerate(both(lhs_halo, wib, a, b)):
+            row = 0
+            for _, n, sy, i in pieces:
+                size = sy.stop - sy.start
+                inner[z, pl.ds(i, n), sy.start - b : sy.stop - b] += term[
+                    row : row + n * size * 8
+                ].reshape(n, size, 8, 256)
+                row += n * size * 8
+
+    def present(i, edge):
+        return jnp.where(i == edge, 0.0, 1.0).astype(F32)
+
+    scale_x = {0: present(ix, 0), groups_x + 1: present(ix, nx - 1)}
+    scale_y = {0: present(iy, 0), groups_y + 1: present(iy, ny - 1)}
+
+    def activate(rows):
+        for i in rows:
+            for z in range(2):
+                row = leaky(inner[z, i]).astype(BF).astype(F32)
+                if i in scale_x:
+                    row = row * scale_x[i]
+                inner[z, i] = row
+                for j, scale in scale_y.items():
+                    inner[z, i, j] = row[j] * scale
+
+    own_y = slice(2, 2 + groups_y)
+
+    def surround(cols, near, far, ring, edge, tap, other):
+        for b in range(3):
+            inside = [j for j in cols if b <= j < b + groups_y + 2]
+            for a in (1, tap, other):
+                pieces = []
+                if inside:
+                    strip = slice(inside[0], inside[-1] + 1)
+                    pieces.append((a, groups_x + 2, strip, 0))
+                if a is tap:
+                    pieces += [(near, 1, own_y, edge), (far, 1, own_y, ring)]
+                elif a is not other:
+                    pieces.append((near, 1, own_y, ring))
+                if pieces:
+                    add(a, b, pieces)
+
     for a in (1, 0, 2):
         load_wo[a].wait()
-        for b in (1, 0, 2):
-            lhs = jnp.concatenate(
+    for d in (2, 4, 6, 8):
+        receive(d)
+    receive(1, core == 0)
+    receive(0, core == 1)
+    surround((0, 1), near_in, far_in, ring_in, edge_in_x, tap_in, tap_out)
+    for d in range(10):
+
+        @pl.when(exists(d))
+        def _():
+            copy_of(d, False).wait_send()
+
+    for d in (3, 5, 7, 9):
+        receive(d)
+    receive(0, core == 0)
+    receive(1, core == 1)
+    surround(
+        (groups_y + 2, groups_y + 3),
+        near_out, far_out, ring_out, edge_out_x, tap_out, tap_in,
+    )
+    activate(range(groups_x + 2))
+    totals = [
+        halo[z, 2 : 2 + groups_x, own_y].reshape(half, 256) + bob[...] for z in range(2)
+    ]
+    for a in range(3):
+        for b in range(3):
+            lhs_in = jnp.concatenate(
                 [
                     inner[z, a : a + groups_x, b : b + groups_y].reshape(half, 256).astype(BF)
                     for z in range(2)
                 ],
                 axis=1,
             )
-            totals = [t + term for t, term in zip(totals, both(lhs, wob, a, b))]
+            totals = [t + term for t, term in zip(totals, both(lhs_in, wob, a, b))]
     lower, upper = leaky(totals[0]), leaky(totals[1])
     even_x = jnp.where(keep, lower, pltpu.roll(upper, 2, 0)).astype(BF)
     odd_x = jnp.where(keep, pltpu.roll(lower, half - 2, 0), upper).astype(BF)
@@ -298,12 +349,6 @@
     for i in range(groups_x):
         for p, part in enumerate((even_x, odd_x)):
             out[2 * i + p] = part[i * rows : (i + 1) * rows].reshape(2 * groups_y, 4, 256)
-
-    for d in range(10):
-
-        @pl.when(exists(d))
-        def _():
-            copy_of(d, False).wait_send()
 
 
 def local(
@@ -328,7 +373,7 @@
         in_specs=[any_spec] * 9,
         out_specs=pl.BlockSpec(memory_space=pltpu.VMEM),
         scratch_shapes=[
-            vmem((gx, 8, size_y, size_z, chans), BF),
+            vmem((gx * 2, 4, size_y, size_z, chans), BF),
             vmem(first_weight.shape, BF),
             vmem(second_weight.shape, BF),
             vmem(inner_weight.shape, BF),
@@ -337,6 +382,7 @@
             vmem((1, 256), F32),
             vmem((1, 256), F32),
             vmem((1, 256), F32),
+            vmem((2, 4, gy * 32, 256), BF),
             vmem((gx * 8, 2, gy * 32, 128), F32),
             vmem((cells, 1024), BF),
             vmem((2, gx + 4, gy + 4, 8, 256), F32),
@@ -345,7 +391,7 @@
             vmem((2, gy * 32, 256), BF),
             vmem((8, 64, 256), BF),
             vmem((8, 64, 256), BF),
-            pltpu.SemaphoreType.DMA((gx + 12,)),
+            pltpu.SemaphoreType.DMA((gx * 2 + 12,)),
             pltpu.SemaphoreType.DMA((10,)),
             pltpu.SemaphoreType.DMA((10,)),
         ],

time: 12.4 us -> 11.8 us (0.952)
  Pallas kernels: 11.6 us -> 11 us
    pallas_call x1, Pallas kernels: 11.6 us -> 11 us  [local(): pl.pallas_call(kernel, out_shape=pltpu.VMEM((size_x // 4, size_y // 4, si...]
where the time goes in v2:
time: 11.8 us; the launch traced here: 11.6 us
  Pallas kernels  11 us (93%)
  local copies, waits for them, and re-layouts  0.66 us (6%)
    pallas_call x1, Pallas kernels, local(): pl.pallas_call(kernel, out_shape=pltpu.VMEM((size_x // 4, size_y // 4, si...  11 us
    unnamed x1, local copies, waits for them, and re-layouts  0.66 us

profile of v2, /device:TPU:0, one launch (start us, length us, event | category | flops | bytes accessed | tf_op | source)
XLA Modules:
  0.0 11.6 jit_solution(5752988185249133210)
XLA Ops:
  0.0 11.0 %shard_map.91 = bf16[8,8,4,256]{3,2,1,0:T(4,128)(2,1)S(1)} custom-call(bf16[32,32,16,64]{3,2,1,0:T(8,128)(2,1)} %volume.1, bf16[2,2,2,64,128]{4,3,2,1,0:T(8,128)(2,1)} %w1.1, f32[1,128]{1,0:T(1,128)} %bitcast.7, bf16[2,2,2,128,256]{4,3,2,1,0:T(8,128)(2,1)} %w2.1, f32[1,256]{1,0:T(1,128)} %bitcast.4, bf16[3,3,3,256,256]{4,3,2,1,0:T(8,128)(2,1)} %wi.1, ...), custom_call_target="tpu_custom_call" | custom-call | flops 2000000000 | bytes 12000000 | tf_op jit(solution)/shard_map/pallas_call | solution.py:370
  11.0 0.7 %copy.11 = bf16[8,8,4,256]{3,2,1,0:T(4,128)(2,1)} copy(bf16[8,8,4,256]{3,2,1,0:T(4,128)(2,1)S(1)} %shard_map.91) | data formatting | bytes 262144

commit v3 on v2

--- a/solution.py
+++ b/solution.py
@@ -71,8 +71,7 @@
     load_w2, load_b2 = load(w2, w2b), load(b2, b2b)
     load_v += [load(volume.at[pl.ds(4 * u, 4)], vbuf.at[u]) for u in range(units // 2, units)]
     load_bi, load_bo = load(bi, bib), load(bo, bob)
-    load_wi = {a: load(wi.at[a], wib.at[a]) for a in (1, 0, 2)}
-    load_wo = {a: load(wo.at[a], wob.at[a]) for a in (1, 0, 2)}
+    load_wi, load_wo = load(wi, wib), load(wo, wob)
 
     halo[...] = jnp.zeros_like(halo)
 
@@ -214,8 +213,23 @@
             jnp.dot(lhs, upper, preferred_element_type=F32),
         )
 
+    def three(low_half, high_half, weight, a, b):
+        shared = (low_half + high_half).astype(BF)
+        return (
+            jnp.dot(shared, weight[a, b, 1], preferred_element_type=F32),
+            jnp.dot(high_half.astype(BF), weight[a, b, 2], preferred_element_type=F32),
+            jnp.dot(low_half.astype(BF), weight[a, b, 0], preferred_element_type=F32),
+        )
+
+    def differences(weight):
+        for a in range(3):
+            for b in range(3):
+                middle = weight[a, b, 1]
+                weight[a, b, 0] = weight[a, b, 0] - middle
+                weight[a, b, 2] = weight[a, b, 2] - middle
+
+    load_wi.wait()
     for a in (1, 0, 2):
-        load_wi[a].wait()
         for b in (1, 0, 2):
             for z, term in enumerate(both(own, wib, a, b)):
                 inner[z, 2 - a : 2 - a + groups_x, 2 - b : 2 - b + groups_y] += term.reshape(
@@ -255,17 +269,15 @@
     near_out, far_out, ring_out, edge_out_x, tap_out = side(1 - core)
 
     def add(a, b, pieces):
-        lhs_halo = jnp.concatenate(
-            [
-                jnp.concatenate(
-                    [halo[z, pl.ds(g, n), sy].reshape(-1, 256) for g, n, sy, _ in pieces],
-                    axis=0,
-                ).astype(BF)
-                for z in range(2)
-            ],
-            axis=1,
-        )
-        for z, term in enumerate(both(lhs_halo, wib, a, b)):
+        halves = [
+            jnp.concatenate(
+                [halo[z, pl.ds(g, n), sy].reshape(-1, 256) for g, n, sy, _ in pieces], axis=0
+            )
+            for z in range(2)
+        ]
+        shared, lower_only, upper_only = three(*halves, wib, a, b)
+        for z, only in enumerate((lower_only, upper_only)):
+            term = shared + only
             row = 0
             for _, n, sy, i in pieces:
                 size = sy.stop - sy.start
@@ -307,8 +319,9 @@
                 if pieces:
                     add(a, b, pieces)
 
-    for a in (1, 0, 2):
-        load_wo[a].wait()
+    load_wo.wait()
+    differences(wib)
+    differences(wob)
     for d in (2, 4, 6, 8):
         receive(d)
     receive(1, core == 0)
@@ -329,19 +342,25 @@
         near_out, far_out, ring_out, edge_out_x, tap_out, tap_in,
     )
     activate(range(groups_x + 2))
+    chains = [None] * 4
+    for tap in range(9):
+        a, b = tap // 3, tap % 3
+        low_half, high_half = [
+            inner[z, a : a + groups_x, b : b + groups_y].reshape(half, 256) for z in range(2)
+        ]
+        shared = low_half + high_half
+        for k, lhs_in, c in (
+            (0, high_half, 2),
+            (1, low_half, 0),
+            (2 + tap % 2, shared, 1),
+        ):
+            term = jnp.dot(lhs_in.astype(BF), wob[a, b, c], preferred_element_type=F32)
+            chains[k] = term if chains[k] is None else chains[k] + term
+    base = chains[2] + chains[3] * present(ix, -1) + bob[...]
     totals = [
-        halo[z, 2 : 2 + groups_x, own_y].reshape(half, 256) + bob[...] for z in range(2)
+        halo[z, 2 : 2 + groups_x, own_y].reshape(half, 256) + base + chains[z]
+        for z in range(2)
     ]
-    for a in range(3):
-        for b in range(3):
-            lhs_in = jnp.concatenate(
-                [
-                    inner[z, a : a + groups_x, b : b + groups_y].reshape(half, 256).astype(BF)
-                    for z in range(2)
-                ],
-                axis=1,
-            )
-            totals = [t + term for t, term in zip(totals, both(lhs_in, wob, a, b))]
     lower, upper = leaky(totals[0]), leaky(totals[1])
     even_x = jnp.where(keep, lower, pltpu.roll(upper, 2, 0)).astype(BF)
     odd_x = jnp.where(keep, pltpu.roll(lower, half - 2, 0), upper).astype(BF)
@@ -391,7 +410,7 @@
             vmem((2, gy * 32, 256), BF),
             vmem((8, 64, 256), BF),
             vmem((8, 64, 256), BF),
-            pltpu.SemaphoreType.DMA((gx * 2 + 12,)),
+            pltpu.SemaphoreType.DMA((gx * 2 + 8,)),
             pltpu.SemaphoreType.DMA((10,)),
             pltpu.SemaphoreType.DMA((10,)),
         ],

time: 11.8 us -> 11.5 us (0.975)
  Pallas kernels: 11 us -> 10.7 us
    pallas_call x1, Pallas kernels: 11 us -> 10.7 us  [local(): pl.pallas_call(kernel, out_shape=pltpu.VMEM((size_x // 4, size_y // 4, si...]
where the time goes in v3:
time: 11.5 us; the launch traced here: 11.4 us
  Pallas kernels  10.7 us (93%)
  local copies, waits for them, and re-layouts  0.66 us (6%)
    pallas_call x1, Pallas kernels, local(): pl.pallas_call(kernel, out_shape=pltpu.VMEM((size_x // 4, size_y // 4, si...  10.7 us
    unnamed x1, local copies, waits for them, and re-layouts  0.66 us

profile of v3, /device:TPU:0, one launch (start us, length us, event | category | flops | bytes accessed | tf_op | source)
XLA Modules:
  0.0 11.4 jit_solution(13769938436239172299)
XLA Ops:
  0.0 10.7 %shard_map.91 = bf16[8,8,4,256]{3,2,1,0:T(4,128)(2,1)S(1)} custom-call(bf16[32,32,16,64]{3,2,1,0:T(8,128)(2,1)} %volume.1, bf16[2,2,2,64,128]{4,3,2,1,0:T(8,128)(2,1)} %w1.1, f32[1,128]{1,0:T(1,128)} %bitcast.7, bf16[2,2,2,128,256]{4,3,2,1,0:T(8,128)(2,1)} %w2.1, f32[1,256]{1,0:T(1,128)} %bitcast.4, bf16[3,3,3,256,256]{4,3,2,1,0:T(8,128)(2,1)} %wi.1, ...), custom_call_target="tpu_custom_call" | custom-call | flops 2000000000 | bytes 12000000 | tf_op jit(solution)/shard_map/pallas_call | solution.py:389
  10.7 0.7 %copy.11 = bf16[8,8,4,256]{3,2,1,0:T(4,128)(2,1)} copy(bf16[8,8,4,256]{3,2,1,0:T(4,128)(2,1)S(1)} %shard_map.91) | data formatting | bytes 262144

commit v4 on v3

--- a/solution.py
+++ b/solution.py
@@ -19,7 +19,7 @@
 
 
 def leaky(values):
-    return jnp.where(values > 0, values, 0.01 * values)
+    return jnp.maximum(values, 0.01 * values)
 
 
 def kernel(
@@ -34,6 +34,11 @@
     groups_x, groups_y = halo.shape[1] - 4, halo.shape[2] - 4
     half = groups_x * groups_y * 8
 
+    def present(i, edge):
+        return jnp.where(i == edge, 0.0, 1.0).astype(F32)
+
+    one = present(ix, -1)
+
     def exists(d):
         dx, dy, _ = MESSAGES[d]
         test = None
@@ -67,9 +72,9 @@
 
     load_w1, load_b1 = load(w1, w1b), load(b1, b1b)
     units = vbuf.shape[0]
-    load_v = [load(volume.at[pl.ds(4 * u, 4)], vbuf.at[u]) for u in range(units // 2)]
+    load_v = [load(volume.at[u], vbuf.at[u]) for u in range(units // 2)]
     load_w2, load_b2 = load(w2, w2b), load(b2, b2b)
-    load_v += [load(volume.at[pl.ds(4 * u, 4)], vbuf.at[u]) for u in range(units // 2, units)]
+    load_v += [load(volume.at[u], vbuf.at[u]) for u in range(units // 2, units)]
     load_bi, load_bo = load(bi, bib), load(bo, bob)
     load_wi, load_wo = load(wi, wib), load(wo, wob)
 
@@ -92,7 +97,7 @@
         slabs = [vbuf[u, j].reshape(rows_y, 4, 16, 64) for j in range(4)]
         for pc in range(2):
             for qc in range(2):
-                lhs[u % 2, pc * 2 + qc] = jnp.concatenate(
+                lhs[u % 4, pc * 2 + qc] = jnp.concatenate(
                     [
                         slabs[2 * pc + p][:, 2 * qc + q].reshape(rows_y * 16, 64)
                         for p in range(2)
@@ -103,7 +108,7 @@
 
     def multiply(u):
         for k in range(4):
-            both = jnp.dot(lhs[u % 2, k], w1cat, preferred_element_type=F32)
+            both = jnp.dot(lhs[u % 4, k], w1cat, preferred_element_type=F32)
             sums[u * 4 + k, 0] = both[:, 0:128]
             sums[u * 4 + k, 1] = both[:, 128:256]
 
@@ -141,27 +146,34 @@
             return px, slice(0, 2) if dy < 0 else slice(groups_y + 2, groups_y + 4)
         return px, slice(2, 2 + groups_y)
 
+    keep = (lax.broadcasted_iota(jnp.int32, (1, 8, 256), 1) // 2) % 2 == 0
+
     def second(h):
         rows = half
-        total = jnp.dot(
-            blocks[h * rows : h * rows + rows],
-            w2b[...].reshape(8 * 128, 256),
-            preferred_element_type=F32,
-        )
+        part = [
+            jnp.dot(
+                blocks[h * rows : h * rows + rows, k * 512 : k * 512 + 512],
+                w2b[k].reshape(4 * 128, 256),
+                preferred_element_type=F32,
+            )
+            for k in range(2)
+        ]
+        total = part[0] + part[1] * one
         coarse = leaky(total + b2b[...]).astype(BF).astype(F32)
         coarse = coarse.reshape(groups_x // 2, 2, groups_y * 8, 256)
-        rows = half // 2
-        even_x = coarse[:, 0].reshape(rows, 256)
-        odd_x = coarse[:, 1].reshape(rows, 256)
-        keep = (lax.broadcasted_iota(jnp.int32, (rows, 256), 0) // 2) % 2 == 0
+        even_x = coarse[:, 0].reshape(-1, 8, 256)
+        odd_x = coarse[:, 1].reshape(-1, 8, 256)
         parts = [
             part.reshape(groups_x // 2, groups_y, 8, 256)
             for part in (
-                jnp.where(keep, even_x, pltpu.roll(odd_x, 2, 0)),
-                jnp.where(keep, pltpu.roll(even_x, rows - 2, 0), odd_x),
+                jnp.where(keep, even_x, pltpu.roll(odd_x, 2, 1)),
+                jnp.where(keep, pltpu.roll(even_x, 6, 1), odd_x),
             )
         ]
-        for d in SECOND if h else FIRST:
+        for z in range(2):
+            halo[z, 2 + 2 * h : 4 + 2 * h, 2 : 2 + groups_y] = parts[z]
+        messages = SECOND if h else FIRST
+        for d in messages:
             dy = MESSAGES[d][1]
             sy = slice(0, 2) if dy < 0 else slice(groups_y - 2, groups_y) if dy else slice(0, groups_y)
             block = jnp.concatenate([p[:, sy].reshape(-1, 256) for p in parts], axis=0).astype(BF)
@@ -169,29 +181,33 @@
                 edge_out[d] = block
             else:
                 corner_out[d - 2] = block
+        if not h:
+            pl.semaphore_wait(barrier, count)
+        for d in messages:
 
             @pl.when(exists(d))
             def _():
                 copy_of(d, False).start()
 
-        for z in range(2):
-            halo[z, 2 + 2 * h : 4 + 2 * h, 2 : 2 + groups_y] = parts[z]
-
-    for t in range(units + 2):
-        if t < units:
-            load_v[t].wait()
-            gather(t)
-        if 1 <= t <= units:
-            multiply(t - 1)
-        if 2 <= t:
-            fold(t - 2)
-        if t == units // 2 + 1:
+    per_half = units // 2
+    for h in range(2):
+        rows = range(h * per_half, (h + 1) * per_half)
+        early = rows[: per_half // 2] if h == 0 else rows
+        for u in early:
+            load_v[u].wait()
+        for u in early:
+            gather(u)
+        for u in rows[len(early) :]:
+            load_v[u].wait()
+        if h == 0:
             load_w2.wait()
             load_b2.wait()
-            pl.semaphore_wait(barrier, count)
-            second(0)
-        if t == units + 1:
-            second(1)
+        for u in rows[len(early) :]:
+            gather(u)
+        for u in rows:
+            multiply(u)
+            fold(u)
+        second(h)
 
     own = jnp.concatenate(
         [
@@ -200,7 +216,6 @@
         ],
         axis=1,
     )
-    keep = (lax.broadcasted_iota(jnp.int32, (half, 256), 0) // 2) % 2 == 0
     load_bi.wait()
     load_bo.wait()
     inner[...] = jnp.broadcast_to(bib[...].reshape(1, 1, 1, 1, 256), inner.shape)
@@ -211,14 +226,6 @@
         return (
             jnp.dot(lhs, lower, preferred_element_type=F32),
             jnp.dot(lhs, upper, preferred_element_type=F32),
-        )
-
-    def three(low_half, high_half, weight, a, b):
-        shared = (low_half + high_half).astype(BF)
-        return (
-            jnp.dot(shared, weight[a, b, 1], preferred_element_type=F32),
-            jnp.dot(high_half.astype(BF), weight[a, b, 2], preferred_element_type=F32),
-            jnp.dot(low_half.astype(BF), weight[a, b, 0], preferred_element_type=F32),
         )
 
     def differences(weight):
@@ -265,19 +272,21 @@
             pick(2, 0),
         )
 
-    near_in, far_in, ring_in, edge_in_x, tap_in = side(core)
-    near_out, far_out, ring_out, edge_out_x, tap_out = side(1 - core)
+    side_in, side_out = side(core), side(1 - core)
+    tap_in, tap_out = side_in[-1], side_out[-1]
 
     def add(a, b, pieces):
-        halves = [
-            jnp.concatenate(
-                [halo[z, pl.ds(g, n), sy].reshape(-1, 256) for g, n, sy, _ in pieces], axis=0
-            )
-            for z in range(2)
-        ]
-        shared, lower_only, upper_only = three(*halves, wib, a, b)
-        for z, only in enumerate((lower_only, upper_only)):
-            term = shared + only
+        lhs_halo = jnp.concatenate(
+            [
+                jnp.concatenate(
+                    [halo[z, pl.ds(g, n), sy].reshape(-1, 256) for g, n, sy, _ in pieces],
+                    axis=0,
+                ).astype(BF)
+                for z in range(2)
+            ],
+            axis=1,
+        )
+        for z, term in enumerate(both(lhs_halo, wib, a, b)):
             row = 0
             for _, n, sy, i in pieces:
                 size = sy.stop - sy.start
@@ -286,62 +295,76 @@
                 ].reshape(n, size, 8, 256)
                 row += n * size * 8
 
-    def present(i, edge):
-        return jnp.where(i == edge, 0.0, 1.0).astype(F32)
-
-    scale_x = {0: present(ix, 0), groups_x + 1: present(ix, nx - 1)}
-    scale_y = {0: present(iy, 0), groups_y + 1: present(iy, ny - 1)}
-
-    def activate(rows):
-        for i in rows:
-            for z in range(2):
-                row = leaky(inner[z, i]).astype(BF).astype(F32)
-                if i in scale_x:
-                    row = row * scale_x[i]
-                inner[z, i] = row
-                for j, scale in scale_y.items():
-                    inner[z, i, j] = row[j] * scale
+    low_there, high_there = present(iy, 0), present(iy, ny - 1)
+    out_there = jnp.where(core == 0, present(ix, 0), present(ix, nx - 1))
+
+    def activate(x, cols, factor=None):
+        for z in range(2):
+            block = leaky(inner[z, x, cols]).astype(BF).astype(F32)
+            if factor is not None:
+                block = block * factor
+            for j in range(cols.start, cols.stop):
+                edge = {0: low_there, groups_y + 1: high_there}.get(j)
+                value = block[j - cols.start]
+                inner[z, x, j] = value if edge is None else value * edge
 
     own_y = slice(2, 2 + groups_y)
 
-    def surround(cols, near, far, ring, edge, tap, other):
-        for b in range(3):
-            inside = [j for j in cols if b <= j < b + groups_y + 2]
-            for a in (1, tap, other):
-                pieces = []
-                if inside:
-                    strip = slice(inside[0], inside[-1] + 1)
-                    pieces.append((a, groups_x + 2, strip, 0))
-                if a is tap:
-                    pieces += [(near, 1, own_y, edge), (far, 1, own_y, ring)]
-                elif a is not other:
-                    pieces.append((near, 1, own_y, ring))
-                if pieces:
-                    add(a, b, pieces)
+    def taps(b, inside, edge_of, roles):
+        near, far, ring, edge, tap = edge_of
+        for a in roles:
+            pieces = []
+            if inside:
+                strip = slice(inside[0], inside[-1] + 1)
+                pieces.append((a, groups_x + 2, strip, 0))
+            if a is tap:
+                pieces += [(near, 1, own_y, edge), (far, 1, own_y, ring)]
+            elif isinstance(a, int):
+                pieces.append((near, 1, own_y, ring))
+            add(a, b, pieces)
 
     load_wo.wait()
-    differences(wib)
     differences(wob)
     for d in (2, 4, 6, 8):
         receive(d)
     receive(1, core == 0)
     receive(0, core == 1)
-    surround((0, 1), near_in, far_in, ring_in, edge_in_x, tap_in, tap_out)
+    taps(0, (0, 1), side_in, (1, tap_in, tap_out))
+    taps(1, (1,), side_in, (1, tap_in, tap_out))
+    taps(2, (), side_in, (1, tap_in))
     for d in range(10):
 
         @pl.when(exists(d))
         def _():
             copy_of(d, False).wait_send()
 
+    settled = 2 * (1 - core)
+    for i in range(groups_x):
+        activate(settled + i, slice(0, groups_y))
+    for z in range(2):
+        halo[z, 2 : 2 + groups_x, own_y] = halo[z, 2 : 2 + groups_x, own_y] + bob[...].reshape(
+            1, 1, 1, 256
+        )
+    receive(0, core == 0)
+    receive(1, core == 1)
+
+    @pl.when(jnp.where(core == 0, ix, nx - 1 - ix) > 0)
+    def _():
+        taps(0, (), side_out, (1, tap_out))
+
     for d in (3, 5, 7, 9):
         receive(d)
-    receive(0, core == 0)
-    receive(1, core == 1)
-    surround(
-        (groups_y + 2, groups_y + 3),
-        near_out, far_out, ring_out, edge_out_x, tap_out, tap_in,
-    )
-    activate(range(groups_x + 2))
+    taps(1, (groups_y + 2,), side_out, (1, tap_out, tap_in))
+    taps(2, (groups_y + 2, groups_y + 3), side_out, (1, tap_out, tap_in))
+    for i in range(groups_x):
+        activate(settled + i, slice(groups_y, groups_y + 2))
+    open_x = groups_x * core
+    for i in range(2):
+        activate(
+            open_x + i,
+            slice(0, groups_y + 2),
+            jnp.where(core == i, out_there, 1.0).astype(F32),
+        )
     chains = [None] * 4
     for tap in range(9):
         a, b = tap // 3, tap % 3
@@ -356,14 +379,14 @@
         ):
             term = jnp.dot(lhs_in.astype(BF), wob[a, b, c], preferred_element_type=F32)
             chains[k] = term if chains[k] is None else chains[k] + term
-    base = chains[2] + chains[3] * present(ix, -1) + bob[...]
+    base = chains[2] + chains[3] * one
     totals = [
         halo[z, 2 : 2 + groups_x, own_y].reshape(half, 256) + base + chains[z]
         for z in range(2)
     ]
-    lower, upper = leaky(totals[0]), leaky(totals[1])
-    even_x = jnp.where(keep, lower, pltpu.roll(upper, 2, 0)).astype(BF)
-    odd_x = jnp.where(keep, pltpu.roll(lower, half - 2, 0), upper).astype(BF)
+    lower, upper = [leaky(t).reshape(-1, 8, 256) for t in totals]
+    even_x = jnp.where(keep, lower, pltpu.roll(upper, 2, 1)).reshape(half, 256).astype(BF)
+    odd_x = jnp.where(keep, pltpu.roll(lower, 6, 1), upper).reshape(half, 256).astype(BF)
     rows = groups_y * 8
     for i in range(groups_x):
         for p, part in enumerate((even_x, odd_x)):
@@ -401,7 +424,7 @@
             vmem((1, 256), F32),
             vmem((1, 256), F32),
             vmem((1, 256), F32),
-            vmem((2, 4, gy * 32, 256), BF),
+            vmem((4, 4, gy * 32, 256), BF),
             vmem((gx * 8, 2, gy * 32, 128), F32),
             vmem((cells, 1024), BF),
             vmem((2, gx + 4, gy + 4, 8, 256), F32),
@@ -421,7 +444,7 @@
             flops=2_000_000_000, bytes_accessed=12_000_000, transcendentals=0
         ),
     )(
-        volume,
+        volume.reshape(gx * 2, 4, size_y, size_z, chans),
         first_weight,
         first_bias.reshape(1, -1),
         second_weight,

time: 11.5 us -> 11.1 us (0.965)
  Pallas kernels: 10.7 us -> 10.3 us
    pallas_call x1, Pallas kernels: 10.7 us -> 10.3 us  [local(): pl.pallas_call(kernel, out_shape=pltpu.VMEM((size_x // 4, size_y // 4, si...]
where the time goes in v4:
time: 11.1 us; the launch traced here: 10.9 us
  Pallas kernels  10.3 us (93%)
  local copies, waits for them, and re-layouts  0.66 us (6%)
    pallas_call x1, Pallas kernels, local(): pl.pallas_call(kernel, out_shape=pltpu.VMEM((size_x // 4, size_y // 4, si...  10.3 us
    unnamed x1, local copies, waits for them, and re-layouts  0.66 us

profile of v4, /device:TPU:0, one launch (start us, length us, event | category | flops | bytes accessed | tf_op | source)
XLA Modules:
  0.0 10.9 jit_solution(5108413537274487059)
XLA Ops:
  0.0 10.3 %shard_map.91 = bf16[8,8,4,256]{3,2,1,0:T(4,128)(2,1)S(1)} custom-call(bf16[8,4,32,16,64]{4,3,2,1,0:T(8,128)(2,1)} %bitcast.5, bf16[2,2,2,64,128]{4,3,2,1,0:T(8,128)(2,1)} %w1.1, f32[1,128]{1,0:T(1,128)} %bitcast.9, bf16[2,2,2,128,256]{4,3,2,1,0:T(8,128)(2,1)} %w2.1, f32[1,256]{1,0:T(1,128)} %bitcast.6, bf16[3,3,3,256,256]{4,3,2,1,0:T(8,128)(2,1)} %wi.1, ...), custom_call_target="tpu_custom_call" | custom-call | flops 2000000000 | bytes 12000000 | tf_op jit(solution)/shard_map/pallas_call | solution.py:412
  10.3 0.7 %copy.11 = bf16[8,8,4,256]{3,2,1,0:T(4,128)(2,1)} copy(bf16[8,8,4,256]{3,2,1,0:T(4,128)(2,1)S(1)} %shard_map.91) | data formatting | bytes 262144

commit v5 on v4

--- a/solution.py
+++ b/solution.py
@@ -189,24 +189,25 @@
             def _():
                 copy_of(d, False).start()
 
-    per_half = units // 2
+    half_units = units // 2
+    quarters = [range(k * units // 4, (k + 1) * units // 4) for k in range(4)]
+
+    def take(rows):
+        for u in rows:
+            load_v[u].wait()
+        for u in rows:
+            gather(u)
+
+    take(quarters[0])
     for h in range(2):
-        rows = range(h * per_half, (h + 1) * per_half)
-        early = rows[: per_half // 2] if h == 0 else rows
-        for u in early:
-            load_v[u].wait()
-        for u in early:
-            gather(u)
-        for u in rows[len(early) :]:
-            load_v[u].wait()
+        take(quarters[2 * h + 1])
+        for u in range(h * half_units, (h + 1) * half_units):
+            multiply(u)
+            fold(u)
         if h == 0:
             load_w2.wait()
             load_b2.wait()
-        for u in rows[len(early) :]:
-            gather(u)
-        for u in rows:
-            multiply(u)
-            fold(u)
+            take(quarters[2])
         second(h)
 
     own = jnp.concatenate(
@@ -325,13 +326,13 @@
 
     load_wo.wait()
     differences(wob)
+    receive(1, core == 0)
+    receive(0, core == 1)
+    taps(2, (), side_in, (1, tap_in))
     for d in (2, 4, 6, 8):
         receive(d)
-    receive(1, core == 0)
-    receive(0, core == 1)
     taps(0, (0, 1), side_in, (1, tap_in, tap_out))
     taps(1, (1,), side_in, (1, tap_in, tap_out))
-    taps(2, (), side_in, (1, tap_in))
     for d in range(10):
 
         @pl.when(exists(d))

time: 11.1 us -> 11.1 us (level)
  the two profiles are of different devices: /device:TPU:0 before, /device:TPU:20 now
where the time goes in v5:
time: 11.1 us; the launch traced here: 10.9 us
  Pallas kernels  10.2 us (92%)
  local copies, waits for them, and re-layouts  0.66 us (6%)
    pallas_call x1, Pallas kernels, local(): pl.pallas_call(kernel, out_shape=pltpu.VMEM((size_x // 4, size_y // 4, si...  10.2 us
    unnamed x1, local copies, waits for them, and re-layouts  0.66 us

profile of v5, /device:TPU:20, one launch (start us, length us, event | category | flops | bytes accessed | tf_op | source)
XLA Modules:
  0.0 10.9 jit_solution(5645137189406029816)
XLA Ops:
  0.0 10.2 %shard_map.91 = bf16[8,8,4,256]{3,2,1,0:T(4,128)(2,1)S(1)} custom-call(bf16[8,4,32,16,64]{4,3,2,1,0:T(8,128)(2,1)} %bitcast.5, bf16[2,2,2,64,128]{4,3,2,1,0:T(8,128)(2,1)} %w1.1, f32[1,128]{1,0:T(1,128)} %bitcast.9, bf16[2,2,2,128,256]{4,3,2,1,0:T(8,128)(2,1)} %w2.1, f32[1,256]{1,0:T(1,128)} %bitcast.6, bf16[3,3,3,256,256]{4,3,2,1,0:T(8,128)(2,1)} %wi.1, ...), custom_call_target="tpu_custom_call" | custom-call | flops 2000000000 | bytes 12000000 | tf_op jit(solution)/shard_map/pallas_call | solution.py:413
  10.2 0.7 %copy.11 = bf16[8,8,4,256]{3,2,1,0:T(4,128)(2,1)} copy(bf16[8,8,4,256]{3,2,1,0:T(4,128)(2,1)S(1)} %shard_map.91) | data formatting | bytes 262144

commit v6 on v5

--- a/solution.py
+++ b/solution.py
@@ -31,6 +31,7 @@
 ):
     ix, iy = lax.axis_index("tx"), lax.axis_index("ty")
     nx, ny = lax.axis_size("tx"), lax.axis_size("ty")
+    core = lax.rem(ix, 2)
     groups_x, groups_y = halo.shape[1] - 4, halo.shape[2] - 4
     half = groups_x * groups_y * 8
 
@@ -72,9 +73,10 @@
 
     load_w1, load_b1 = load(w1, w1b), load(b1, b1b)
     units = vbuf.shape[0]
-    load_v = [load(volume.at[u], vbuf.at[u]) for u in range(units // 2)]
+    quarters = [pl.ds(k * units // 4, units // 4) for k in range(4)]
+    load_v = [load(volume.at[q], vbuf.at[q]) for q in quarters[:2]]
     load_w2, load_b2 = load(w2, w2b), load(b2, b2b)
-    load_v += [load(volume.at[u], vbuf.at[u]) for u in range(units // 2, units)]
+    load_v += [load(volume.at[q], vbuf.at[q]) for q in quarters[2:]]
     load_bi, load_bo = load(bi, bib), load(bo, bob)
     load_wi, load_wo = load(wi, wib), load(wo, wob)
 
@@ -147,6 +149,15 @@
         return px, slice(2, 2 + groups_y)
 
     keep = (lax.broadcasted_iota(jnp.int32, (1, 8, 256), 1) // 2) % 2 == 0
+
+    def send(d, test=None):
+        there = exists(d)
+        if test is not None:
+            there = jnp.logical_and(there, test)
+
+        @pl.when(there)
+        def _():
+            copy_of(d, False).start()
 
     def second(h):
         rows = half
@@ -183,31 +194,29 @@
                 corner_out[d - 2] = block
         if not h:
             pl.semaphore_wait(barrier, count)
-        for d in messages:
-
-            @pl.when(exists(d))
-            def _():
-                copy_of(d, False).start()
+        edge, rest = messages[-1], messages[:-1]
+        send(edge, core == edge)
+        for d in rest:
+            send(d)
+        send(edge, core == 1 - edge)
 
     half_units = units // 2
-    quarters = [range(k * units // 4, (k + 1) * units // 4) for k in range(4)]
-
-    def take(rows):
-        for u in rows:
-            load_v[u].wait()
-        for u in rows:
+
+    def take(k):
+        load_v[k].wait()
+        for u in range(k * units // 4, (k + 1) * units // 4):
             gather(u)
 
-    take(quarters[0])
+    take(0)
     for h in range(2):
-        take(quarters[2 * h + 1])
+        take(2 * h + 1)
         for u in range(h * half_units, (h + 1) * half_units):
             multiply(u)
             fold(u)
         if h == 0:
             load_w2.wait()
             load_b2.wait()
-            take(quarters[2])
+            take(2)
         second(h)
 
     own = jnp.concatenate(
@@ -258,8 +267,6 @@
             for z in range(2):
                 shape = (px.stop - px.start, py.stop - py.start, 8, 256)
                 halo[z, px, py] = block[z * rows : z * rows + rows].reshape(shape)
-
-    core = lax.rem(ix, 2)
 
     def side(flip):
         def pick(even, odd):
@@ -434,7 +441,7 @@
             vmem((2, gy * 32, 256), BF),
             vmem((8, 64, 256), BF),
             vmem((8, 64, 256), BF),
-            pltpu.SemaphoreType.DMA((gx * 2 + 8,)),
+            pltpu.SemaphoreType.DMA((12,)),
             pltpu.SemaphoreType.DMA((10,)),
             pltpu.SemaphoreType.DMA((10,)),
         ],

time: 11.1 us -> 11 us (level)
  the two profiles are of different devices: /device:TPU:20 before, /device:TPU:0 now
where the time goes in v6:
time: 11 us; the launch traced here: 10.8 us
  Pallas kernels  10.2 us (93%)
  local copies, waits for them, and re-layouts  0.66 us (6%)
    pallas_call x1, Pallas kernels, local(): pl.pallas_call(kernel, out_shape=pltpu.VMEM((size_x // 4, size_y // 4, si...  10.2 us
    unnamed x1, local copies, waits for them, and re-layouts  0.66 us

profile of v6, /device:TPU:0, one launch (start us, length us, event | category | flops | bytes accessed | tf_op | source)
XLA Modules:
  0.0 10.8 jit_solution(4998487450410072786)
XLA Ops:
  0.0 10.2 %shard_map.91 = bf16[8,8,4,256]{3,2,1,0:T(4,128)(2,1)S(1)} custom-call(bf16[8,4,32,16,64]{4,3,2,1,0:T(8,128)(2,1)} %bitcast.5, bf16[2,2,2,64,128]{4,3,2,1,0:T(8,128)(2,1)} %w1.1, f32[1,128]{1,0:T(1,128)} %bitcast.9, bf16[2,2,2,128,256]{4,3,2,1,0:T(8,128)(2,1)} %w2.1, f32[1,256]{1,0:T(1,128)} %bitcast.6, bf16[3,3,3,256,256]{4,3,2,1,0:T(8,128)(2,1)} %wi.1, ...), custom_call_target="tpu_custom_call" | custom-call | flops 2000000000 | bytes 12000000 | tf_op jit(solution)/shard_map/pallas_call | solution.py:420
  10.2 0.7 %copy.11 = bf16[8,8,4,256]{3,2,1,0:T(4,128)(2,1)} copy(bf16[8,8,4,256]{3,2,1,0:T(4,128)(2,1)S(1)} %shard_map.91) | data formatting | bytes 262144

commit v7 on v6

--- a/solution.py
+++ b/solution.py
@@ -353,6 +353,8 @@
         halo[z, 2 : 2 + groups_x, own_y] = halo[z, 2 : 2 + groups_x, own_y] + bob[...].reshape(
             1, 1, 1, 256
         )
+    for d in (5, 7):
+        receive(d)
     receive(0, core == 0)
     receive(1, core == 1)
 
@@ -360,10 +362,10 @@
     def _():
         taps(0, (), side_out, (1, tap_out))
 
-    for d in (3, 5, 7, 9):
+    for d in (3, 9):
         receive(d)
+    taps(2, (groups_y + 2, groups_y + 3), side_out, (1, tap_out, tap_in))
     taps(1, (groups_y + 2,), side_out, (1, tap_out, tap_in))
-    taps(2, (groups_y + 2, groups_y + 3), side_out, (1, tap_out, tap_in))
     for i in range(groups_x):
         activate(settled + i, slice(groups_y, groups_y + 2))
     open_x = groups_x * core

time: 11 us -> 11 us (level)
  no operation moved by 1% of the time
where the time goes in v7:
time: 11 us; the launch traced here: 10.8 us
  Pallas kernels  10.2 us (93%)
  local copies, waits for them, and re-layouts  0.66 us (6%)
    pallas_call x1, Pallas kernels, local(): pl.pallas_call(kernel, out_shape=pltpu.VMEM((size_x // 4, size_y // 4, si...  10.2 us
    unnamed x1, local copies, waits for them, and re-layouts  0.66 us

profile of v7, /device:TPU:0, one launch (start us, length us, event | category | flops | bytes accessed | tf_op | source)
XLA Modules:
  0.0 10.8 jit_solution(11627607660742605312)
XLA Ops:
  0.0 10.2 %shard_map.91 = bf16[8,8,4,256]{3,2,1,0:T(4,128)(2,1)S(1)} custom-call(bf16[8,4,32,16,64]{4,3,2,1,0:T(8,128)(2,1)} %bitcast.5, bf16[2,2,2,64,128]{4,3,2,1,0:T(8,128)(2,1)} %w1.1, f32[1,128]{1,0:T(1,128)} %bitcast.9, bf16[2,2,2,128,256]{4,3,2,1,0:T(8,128)(2,1)} %w2.1, f32[1,256]{1,0:T(1,128)} %bitcast.6, bf16[3,3,3,256,256]{4,3,2,1,0:T(8,128)(2,1)} %wi.1, ...), custom_call_target="tpu_custom_call" | custom-call | flops 2000000000 | bytes 12000000 | tf_op jit(solution)/shard_map/pallas_call | solution.py:422
  10.2 0.7 %copy.11 = bf16[8,8,4,256]{3,2,1,0:T(4,128)(2,1)} copy(bf16[8,8,4,256]{3,2,1,0:T(4,128)(2,1)S(1)} %shard_map.91) | data formatting | bytes 262144
